TPU v7x, 256 devices: a whole 4x4x8 slice. The times are simulated.
256 devices in a mesh: ctx: 16 (over x, y_lo, core), dp: 16 (over y_hi, z).
Axes of the slice: x: 4, y: 4 (y_hi: 2, y_lo: 2; y = y_hi * 2 + y_lo), z: 8, core: 2. Of those that a mesh axis runs over, the one named last changes fastest.
Arguments:
- hidden_in: bfloat16 [16, 2048, 7168], P('dp', 'ctx'), may hold values from -6 to 6
- proj_weight: bfloat16 [7168, 576], P('ctx'), may hold values from -0.0625 to 0.0625
- proj_delta: bfloat16 [7168, 576], P('ctx'), may hold values from -0.03125 to 0.03125
- norm_gain: float32 [512], replicated, may hold values from 0.25 to 1.75
- queries: bfloat16 [16, 64, 73728], P('dp', 'ctx'), may hold values from -32 to 32
- out_grad: bfloat16 [16, 64, 65536], P('dp', 'ctx'), may hold values from -6 to 6
- seg_map: int32 [16, 16], P('dp'), may hold values from 0 to 15, each once within a row
Outputs:
- query_grad: bfloat16 [16, 64, 73728], P('dp', 'ctx')
- weight_grad: float32 [7168, 576], P('ctx')
Inputs may be any that keep to these rules, and one draw needn't show every extreme that they name: Each row of seg_map names every segment 0 to 15 exactly once.
All inputs are finite; a program needn't handle non-finite values.
Results may differ from a plain program's by a relative error of at most 0.025.
The roundings to bfloat16 on the way count: a program that leaves them out, or rounds other values in their place, can miss the bound.
Values may be sent and summed in bfloat16 or wider, within the bound.
A program may use at most 128 MiB of HBM per device.

v0:
```python
import jax
import jax.numpy as jnp
import numpy as np
from jax import lax
from jax.experimental import pallas as pl
from jax.experimental.pallas import tpu as pltpu
from jax.sharding import PartitionSpec as P

H = 128
LAT = 512
ROPE = 64
KD = LAT + ROPE
HALF = ROPE // 2
NORM_EPS = 1e-06
SOFT_SCALE = 192.0 ** (-0.5)
ROPE_BASE = 10000.0

NX, NY, NZ = 4, 2, 8
ROWS = 128
NQ = 4
QR = NQ * H
DSH = 448
CHIP = 2 * DSH
D = 16 * DSH
LT = LAT // 128
WF = DSH * KD // 128
KF = ROWS * KD // 128
ZF = 64
W_ONE, W_A, W_B = 736, 544, 736
W_ODD = W_A + W_B
BF = jnp.bfloat16
F32 = jnp.float32
MESH = pl.DeviceIdType.MESH


def dot(a, b):
    return jnp.dot(a, b, preferred_element_type=F32)


def dot_t(a, b):
    return lax.dot_general(a, b, (((1,), (1,)), ((), ())), preferred_element_type=F32)


def t_dot(a, b):
    return lax.dot_general(a, b, (((0,), (0,)), ((), ())), preferred_element_type=F32)


def fold(part):
    n = part.shape[0] // 2
    return jnp.concatenate([part[:n], part[n:]], axis=1)


def unfold(part):
    return jnp.concatenate([part[:, :ROPE], part[:, ROPE:]], axis=0)


RING, KEYS, TWIN, ONCE = 0, 18, 36, 44
N_SEMS = ONCE + 50


class Net:
    def __init__(self, send_sems, recv_sems):
        self.send_sems, self.recv_sems = send_sems, recv_sems
        self.last, self.next = {}, {}

    def reuse(self, pool):
        self.next[pool] = 0

    def send(self, src, dst, to, pool=ONCE):
        i = pool + self.next.get(pool, 0)
        self.next[pool] = i + 1 - pool
        if i in self.last:
            self.last[i].wait_send()
        copy = pltpu.make_async_remote_copy(
            src_ref=src,
            dst_ref=dst,
            send_sem=self.send_sems.at[i],
            recv_sem=self.recv_sems.at[i],
            device_id=to,
            device_id_type=MESH,
        )
        copy.start()
        self.last[i] = copy
        return copy

    def sent(self, *copies):
        for i, copy in list(self.last.items()):
            if any(copy is c for c in copies):
                copy.wait_send()
                del self.last[i]

    def finish(self):
        for i in sorted(self.last):
            self.last[i].wait_send()


def kernel(
    seg_in, hid, w_ref, dw_ref, gain_ref, freq_ref, q_in, g_in,
    qg_out, agz,
    seg, q_raw, g_raw, q_ref, g_ref, own_hid, hidw, hidt, wbuf, acc, prec, unit_ref, inv_ref, trig,
    kflat, kbuf, e_ref, gp_ref, wt_ref, gs_ref, m_ref, l_ref, mj_ref, rd_ref,
    pf, pb, pr, qacc,
    b1s, b1r, a1s, a1r, a2s, a2r, a3s, a3r, b2s, b2r, b3s, b3r, t_b,
    gflat, gbuf, hrecv, h_t, term, tsend, trecv,
    arflat, arz, arl, far_half, near_half, qg_ref,
    send_sems, recv_sems, local_sems,
):
    c, d = lax.axis_index("ctx"), lax.axis_index("dp")
    x, y, core = lax.div(c, 4), lax.rem(lax.div(c, 2), 2), lax.rem(c, 2)
    yh, z = lax.div(d, NZ), lax.rem(d, NZ)
    xr, xl, xo, yo = lax.rem(x + 1, 4), lax.rem(x + 3, 4), lax.rem(x + 2, 4), 1 - y
    sib = 1 - core

    def at(xx, yy, cc=core):
        return {"ctx": xx * 4 + yy * 2 + cc}

    right, left, across, twin = at(xr, y), at(xl, y), at(x, yo), at(x, y, sib)

    def chip(xx, yy):
        return xx * 2 + yy

    others = [(xr, y), (xl, y), (x, yo), (xo, y), (xr, yo), (xl, yo), (xo, yo)]
    senders = [(xl, y), (xr, y), (x, yo), (xo, y), (xl, yo), (xr, yo), (xo, yo)]
    z_up = {"dp": yh * NZ + lax.rem(z + 1, NZ)}
    z_down = {"dp": yh * NZ + lax.rem(z + NZ - 1, NZ)}
    sequences = [
        lax.rem(yh + k // NZ, 2) * NZ + lax.rem(z + k % NZ, NZ) for k in range(1, 2 * NZ)
    ]

    barrier = pltpu.get_barrier_semaphore()
    peers = [right, left, across, twin] + [{"dp": dd} for dd in sequences]
    for peer in peers:
        pl.semaphore_signal(barrier, inc=1, device_id=peer, device_id_type=MESH)
    own_hidden = pltpu.make_async_copy(hid, own_hid, local_sems.at[0])
    own_hidden.start()
    own_queries = pltpu.make_async_copy(q_in, q_raw, local_sems.at[1])
    own_queries.start()
    own_grads = pltpu.make_async_copy(g_in, g_raw, local_sems.at[2])
    own_grads.start()
    own_segments = pltpu.make_async_copy(seg_in, seg, local_sems.at[3])
    own_segments.start()
    perturbed = (w_ref[...].astype(F32) + dw_ref[...].astype(F32)).astype(BF)
    mine = chip(x, y)
    for j in range(LT):
        wbuf[mine, pl.ds(DSH * j, DSH), :] = perturbed[:, 128 * j : 128 * j + 128]
    wbuf[mine, pl.ds(DSH * LT, DSH // 2), :] = fold(perturbed[:, LAT:])
    pl.semaphore_wait(barrier, len(peers))

    net = Net(send_sems, recv_sems)

    def all_gather(pool, buf, slot, base, n_a, n_b, idle, on_block):
        h_a, h_b = n_a // 2, n_b // 2

        def send(xx, yy, lo, n, to):
            ref = buf.at[slot(xx, yy), pl.ds(pl.multiple_of(base + lo, 16), n)]
            return net.send(ref, ref, to, pool)

        a_r = send(x, y, 0, n_a, right)
        a_l = send(x, y, 0, n_a, left)
        b_y = send(x, y, n_a, n_b, across)
        b_r = send(x, y, n_a, n_b, right)
        b_l = send(x, y, n_a, n_b, left)
        a_y = send(x, y, 0, n_a, across)
        idle[0]()
        on_block(x, y)
        b_y.wait_recv()
        bp_r = send(x, yo, n_a, n_b, right)
        bp_l = send(x, yo, n_a, n_b, left)
        a_r.wait_recv()
        a_r2 = send(xl, y, 0, h_a, right)
        a_yl = send(xl, y, 0, n_a, across)
        a_l.wait_recv()
        a_l2 = send(xr, y, h_a, h_a, left)
        a_yr = send(xr, y, 0, n_a, across)
        b_r.wait_recv()
        b_r2 = send(xl, y, n_a, h_b, right)
        b_l.wait_recv()
        b_l2 = send(xr, y, n_a + h_b, h_b, left)
        idle[1]()
        on_block(xl, y)
        on_block(xr, y)
        a_y.wait_recv()
        on_block(x, yo)
        bp_r.wait_recv()
        bp_r2 = send(xl, yo, n_a, h_b, right)
        bp_l.wait_recv()
        bp_l2 = send(xr, yo, n_a + h_b, h_b, left)
        a_r2.wait_recv()
        a_y1 = send(xo, y, 0, h_a, across)
        a_l2.wait_recv()
        a_y2 = send(xo, y, h_a, h_a, across)
        idle[2]()
        a_yl.wait_recv()
        on_block(xl, yo)
        a_yr.wait_recv()
        on_block(xr, yo)
        b_r2.wait_recv()
        b_l2.wait_recv()
        on_block(xo, y)
        bp_r2.wait_recv()
        bp_l2.wait_recv()
        a_y1.wait_recv()
        a_y2.wait_recv()
        on_block(xo, yo)

    def nothing():
        pass

    def angles():
        pos = (seg[0, c] * ROWS + lax.broadcasted_iota(jnp.int32, (ROWS, HALF), 0)).astype(F32)
        angle = pos * freq_ref[...]
        trig[:, :HALF] = jnp.cos(angle)
        trig[:, HALF:] = jnp.sin(angle)
        acc[...] = jnp.zeros_like(acc)

    def heads_to_rows(src, dst, width):
        def body(i, _):
            pieces = []
            for k in range(2):
                lo = pl.multiple_of((2 * i + k) * 2 * width, 128)
                block = src[:, pl.ds(lo, 2 * width)].astype(F32)
                pieces += [block[:, :width], block[:, width:]]
            rows = pl.ds(pl.multiple_of(i * 16, 16), 16)
            dst[rows, :] = jnp.concatenate(pieces, axis=0).astype(BF)
            return 0

        lax.fori_loop(0, QR // 16, body, 0)

    def hidden_windows():
        own_segments.wait()
        angles()
        own_hidden.wait()
        for i in range(NX * NY):
            pad = slice(512 * i + DSH, 512 * i + 512)
            hidw[:ROWS, pad] = jnp.zeros((ROWS, 512 - DSH), BF)
            hidt[:, pad] = jnp.zeros((ROWS, 512 - DSH), BF)

        for cc in range(2):

            @pl.when(core == cc)
            def _():
                for i in range(NX * NY):
                    lo, other = CHIP * i + DSH * cc, CHIP * i + DSH * (1 - cc)
                    hidw[:ROWS, 512 * i : 512 * i + DSH] = own_hid[:, lo : lo + DSH]
                    hidt[:, 512 * i : 512 * i + DSH] = own_hid[:, other : other + DSH]

        twin_hidden.append(net.send(hidt, hidw.at[pl.ds(ROWS, ROWS)], twin))
        hrecv[mine] = own_hid[:, pl.ds(pl.multiple_of(mine * CHIP, 128), CHIP)]

    twin_hidden = []

    def query_rows():
        own_queries.wait()
        heads_to_rows(q_raw, q_ref, KD)

    def grad_rows():
        own_grads.wait()
        heads_to_rows(g_raw, g_ref, LAT)

    def project(xx, yy):
        p = chip(xx, yy)
        lhs = hidw[:, pl.ds(pl.multiple_of(p * 512, 512), DSH)]
        tiles = [wbuf[p, pl.ds(DSH * j, DSH), :] for j in range(LT)]
        for j in range(0, LT, 2):
            acc[:, 128 * j : 128 * j + 256] += dot(
                lhs, jnp.concatenate([tiles[j], tiles[j + 1]], axis=1)
            )
        acc[:, LAT:] += dot(lhs, unfold(wbuf[p, pl.ds(DSH * LT, DSH // 2), :]))

    odd = lax.rem(z, 2)
    from_z = []
    parts = []

    def to_chip(k):
        xx, yy = others[k]
        columns = pl.ds(pl.multiple_of(chip(xx, yy) * CHIP, 128), CHIP)
        parts.append(net.send(own_hid.at[:, columns], hrecv.at[mine], at(xx, yy)))

    def project_next():
        xx, yy, copies = from_z.pop(0)
        for copy in copies:
            copy.wait_recv()
        project(xx, yy)

    def on_weights(xx, yy):
        def send(lo, n, to):
            ref = wbuf.at[chip(xx, yy), pl.ds(pl.multiple_of(odd * W_ODD + lo, 16), n)]
            return net.send(ref, ref, to)

        k = n_blocks[0]
        n_blocks[0] += 1
        if k == 0:
            copies = []
        elif k == 7:
            copies = [send(0, W_ONE // 2, z_up), send(W_ONE // 2, W_ONE // 2, z_down)]
        else:
            copies = [send(0, W_ONE, z_up if k in (1, 3, 4) else z_down)]
        from_z.append((xx, yy, copies))
        if k == 4:
            for i in (0, 1, 2):
                to_chip(i)
            twin_hidden[0].wait_recv()
        if k == 6:
            for i in (4, 5):
                to_chip(i)
        if k >= 4:
            project_next()
        if k == 7:
            while from_z:
                project_next()

    n_blocks = [0]
    idle = (hidden_windows, query_rows, grad_rows)
    all_gather(RING, wbuf, chip, odd * W_ONE, W_A, W_B, idle, on_weights)
    swap = net.send(acc.at[pl.ds(ROWS, ROWS)], prec, twin)
    swap.wait_recv()
    projected = acc[:ROWS, :] + prec[...]

    latent = projected[:, :LAT]
    inverse = lax.rsqrt(jnp.mean(latent * latent, axis=-1, keepdims=True) + NORM_EPS)
    unit = latent * inverse
    unit_ref[...] = unit
    inv_ref[...] = jnp.broadcast_to(inverse, (ROWS, 128))
    key_latent = (unit * gain_ref[...]).astype(BF)
    cosine, sine = trig[:, :HALF], trig[:, HALF:]
    first_half, second_half = projected[:, LAT : LAT + HALF], projected[:, LAT + HALF :]
    key_rope = jnp.concatenate(
        [first_half * cosine - second_half * sine, second_half * cosine + first_half * sine],
        axis=-1,
    )
    for j in range(LT):
        kflat[c, pl.ds(ROWS * j, ROWS), :] = key_latent[:, 128 * j : 128 * j + 128]
    kflat[c, pl.ds(ROWS * LT, ROWS // 2), :] = fold(key_rope).astype(BF)

    def slot(xx, yy):
        return xx * 4 + yy * 2 + core

    waiting = []

    def pair():
        copy, xx, yy = waiting.pop(0)
        copy.wait_recv()
        scores(xx, yy)

    def on_key(xx, yy):
        ref = kflat.at[slot(xx, yy)]
        waiting.append((net.send(ref, ref, twin, TWIN), xx, yy))
        if len(waiting) > 1:
            pair()

    def unpack(flat, rows, lo):
        for j in range(LT):
            rows[pl.ds(lo, ROWS), 128 * j : 128 * j + 128] = flat[pl.ds(ROWS * j, ROWS), :]
        rows[pl.ds(lo, ROWS), LAT:] = unfold(flat[pl.ds(ROWS * LT, ROWS // 2), :])

    def chip_rows(p):
        return pl.ds(pl.multiple_of(p * 256, 256), 256)

    query_pos = (
        seg[0, c] * ROWS
        + (lax.rem(lax.broadcasted_iota(jnp.int32, (1, QR), 1), NQ) + 1) * (ROWS // NQ)
        - 1
    )

    def start_scores():
        m_ref[...] = jnp.full_like(m_ref, -jnp.inf)
        l_ref[...] = jnp.zeros_like(l_ref)

    def scores(xx, yy):
        p = chip(xx, yy)
        for cc in range(2):
            unpack(kflat.at[2 * p + cc], kbuf, pl.multiple_of(p * 256 + 128 * cc, 128))
        rows = chip_rows(p)
        row = lax.broadcasted_iota(jnp.int32, (256, 1), 0)
        key_pos = (
            jnp.where(row < ROWS, seg[0, 2 * p], seg[0, 2 * p + 1]) * ROWS + lax.rem(row, ROWS)
        )
        s = SOFT_SCALE * dot_t(kbuf[rows, :], q_ref[...])
        s = jnp.where(key_pos <= query_pos, s, -jnp.inf)
        old = m_ref[...]
        new = jnp.maximum(old, jnp.max(s, axis=0, keepdims=True))
        e = jnp.exp(s - new)
        e_ref[rows, :] = e
        m_ref[...] = new
        mj_ref[p] = new
        l_ref[...] = l_ref[...] * jnp.exp(old - new) + jnp.sum(e, axis=0, keepdims=True)
        gp_ref[rows, :] = dot_t(kbuf[rows, :LAT], g_ref[...])

    all_gather(KEYS, kflat, slot, 0, 256, 320, (start_scores, nothing, nothing), on_key)

    to_chip(3)
    to_chip(6)
    pair()

    scale_by = 1.0 / l_ref[...]
    top = m_ref[...]
    rd_ref[...] = jnp.zeros_like(rd_ref)
    step = 64

    def weigh(i, _):
        rows = pl.ds(pl.multiple_of(i * step, step), step)
        factor = jnp.exp(mj_ref[lax.div(i, 256 // step)] - top) * scale_by
        weights = (e_ref[rows, :] * factor).astype(BF)
        wt_ref[rows, :] = weights
        rd_ref[...] += jnp.sum(weights.astype(F32) * gp_ref[rows, :], axis=0, keepdims=True)
        return 0

    lax.fori_loop(0, 2048 // step, weigh, 0)

    arrivals = [(x, y), (xl, y), (xr, y), (x, yo), (xl, yo), (xr, yo), (xo, y), (xo, yo)]

    def turn(i):
        if i > 0:
            parts[i - 1].wait_recv()
        h_t[:, 128 * i : 128 * i + 128] = hrecv[chip(*arrivals[i])].T

    def key_gradient(xx, yy, i):
        p = chip(xx, yy)
        rows = chip_rows(p)
        factor = jnp.exp(mj_ref[p] - m_ref[...]) * (SOFT_SCALE / l_ref[...])
        gs = (e_ref[rows, :] * factor * (gp_ref[rows, :] - rd_ref[...])).astype(BF)
        gs_ref[rows, :] = gs
        lat = dot(gs, q_ref[:, :LAT]) + dot(wt_ref[rows, :], g_ref[...])
        rope = dot(gs, q_ref[:, LAT:])
        for cc in range(2):
            half = slice(cc * ROWS, cc * ROWS + ROWS)
            for j in range(LT):
                tile = lat[half, 128 * j : 128 * j + 128]
                pf[i, cc, pl.ds(ROWS * j, ROWS), :] = tile
                pb[i, cc, pl.ds(ROWS * j, ROWS), :] = tile.astype(BF)
            tile = fold(rope[half])
            pf[i, cc, pl.ds(ROWS * LT, ROWS // 2), :] = tile
            pb[i, cc, pl.ds(ROWS * LT, ROWS // 2), :] = tile.astype(BF)
        return net.send(pb.at[i, sib], pr.at[i], twin)

    n_a, n_b = 256, 320
    h_a, h_b = n_a // 2, n_b // 2

    def summed(i, copy):
        copy.wait_recv()
        return pf[i, core] + pr[i].astype(F32)

    order = [(xo, yo), (xo, y), (xl, yo), (xr, yo), (x, yo), (xl, y), (xr, y), (x, y)]
    OO, OY, LO, RO, SO, LY, RY, SY = range(8)
    copies = [key_gradient(*order[0], 0), key_gradient(*order[1], 1)]
    net.reuse(RING)
    sums = {}
    a1 = []
    b1 = []
    for i in range(8):
        if i + 2 < 8:
            copies.append(key_gradient(*order[i + 2], i + 2))
        block = summed(i, copies[i])
        pf[i, core] = block
        if i in (OO, OY):
            yi = 1 if i == OO else 0
            a1s[yi, 0] = block[:h_a].astype(BF)
            a1s[yi, 1] = block[h_a:n_a].astype(BF)
            a1.append(net.send(a1s.at[yi, 0], a1r.at[yi, 0], right, RING))
            a1.append(net.send(a1s.at[yi, 1], a1r.at[yi, 1], left, RING))
        if i in (OO, LO, RO, SO):
            bi = {OO: 0, LO: 1, RO: 2, SO: 3}[i]
            b1s[bi] = block[n_a:].astype(BF)
            b1.append(net.send(b1s.at[bi], b1r.at[bi], across, RING))

    def own(i, lo, n):
        return pf[i, core, pl.ds(lo, n), :]

    def query_gradient():
        qacc[...] = jnp.zeros_like(qacc)

        def body(p, _):
            rows = chip_rows(p)
            qacc[...] += t_dot(gs_ref[rows, :], kbuf[rows, :])
            return 0

        lax.fori_loop(0, NX * NY, body, 0)

    def rows_to_heads():
        def body(i, _):
            rows = qacc[pl.ds(pl.multiple_of(i * 16, 16), 16), :]
            heads = jnp.concatenate([rows[4 * k : 4 * k + 4] for k in range(4)], axis=1)
            qg_ref[:, pl.ds(pl.multiple_of(i * 4 * KD, 128), 4 * KD)] = heads.astype(BF)
            return 0

        lax.fori_loop(0, QR // 16, body, 0)

    b1[0].wait_recv()
    t_b[0] = own(OY, n_a, n_b) + b1r[0].astype(F32)
    b2s[0] = t_b[0, :h_b].astype(BF)
    b2s[1] = t_b[0, h_b:].astype(BF)
    b2 = [net.send(b2s.at[0], b2r.at[0], right, RING), net.send(b2s.at[1], b2r.at[1], left, RING)]
    for copy in a1:
        copy.wait_recv()
    a2 = []
    for yi, (il, ir) in enumerate(((LY, RY), (LO, RO))):
        a2s[yi, 0, :h_a] = (own(ir, 0, h_a) + a1r[yi, 0].astype(F32)).astype(BF)
        a2s[yi, 0, h_a:] = own(ir, h_a, h_a).astype(BF)
        a2s[yi, 1, :h_a] = own(il, 0, h_a).astype(BF)
        a2s[yi, 1, h_a:] = (own(il, h_a, h_a) + a1r[yi, 1].astype(F32)).astype(BF)
        a2.append(net.send(a2s.at[yi, 0], a2r.at[yi, 0], right, RING))
        a2.append(net.send(a2s.at[yi, 1], a2r.at[yi, 1], left, RING))
    for i in range(6):
        turn(i)
    for copy in b1[1:]:
        copy.wait_recv()
    t_b[1] = own(LY, n_a, n_b) + b1r[1].astype(F32)
    t_b[2] = own(RY, n_a, n_b) + b1r[2].astype(F32)
    t_b[3] = own(SY, n_a, n_b) + b1r[3].astype(F32)
    for copy in b2:
        copy.wait_recv()
    b3s[0, :h_b] = (t_b[2, :h_b] + b2r[0].astype(F32)).astype(BF)
    b3s[0, h_b:] = t_b[2, h_b:].astype(BF)
    b3s[1, :h_b] = t_b[1, :h_b].astype(BF)
    b3s[1, h_b:] = (t_b[1, h_b:] + b2r[1].astype(F32)).astype(BF)
    b3 = [net.send(b3s.at[0], b3r.at[0], right, RING), net.send(b3s.at[1], b3r.at[1], left, RING)]
    for copy in a2:
        copy.wait_recv()
    a3s[...] = (own(SO, 0, n_a) + a2r[1, 0].astype(F32) + a2r[1, 1].astype(F32)).astype(BF)
    a3 = net.send(a3s, a3r, across, RING)
    for copy in b3:
        copy.wait_recv()
    grad_b = t_b[3] + b3r[0].astype(F32) + b3r[1].astype(F32)
    a3.wait_recv()
    grad_a = (
        own(SY, 0, n_a)
        + a2r[0, 0].astype(F32)
        + a2r[0, 1].astype(F32)
        + a3r[...].astype(F32)
    )

    grad_latent = jnp.concatenate(
        [grad_a[:ROWS], grad_a[ROWS:], grad_b[:ROWS], grad_b[ROWS : 2 * ROWS]], axis=1
    )
    grad_rope = unfold(grad_b[2 * ROWS :])
    unit = unit_ref[...]
    scaled = grad_latent * gain_ref[...]
    grad_latent = inv_ref[:, :1] * (
        scaled - unit * jnp.mean(scaled * unit, axis=-1, keepdims=True)
    )
    cosine, sine = trig[:, :HALF], trig[:, HALF:]
    upper, lower = grad_rope[:, :HALF], grad_rope[:, HALF:]
    grad_rope = jnp.concatenate(
        [upper * cosine + lower * sine, lower * cosine - upper * sine], axis=-1
    )
    for j in range(LT):
        gflat[c, pl.ds(ROWS * j, ROWS), :] = grad_latent[:, 128 * j : 128 * j + 128].astype(BF)
    gflat[c, pl.ds(ROWS * LT, ROWS // 2), :] = fold(grad_rope).astype(BF)

    blocks = []

    def add_term(xx, yy):
        k = len(blocks)
        blocks.append(k)
        if k >= 6:
            turn(k)
        unpack(gflat.at[slot(xx, yy)], gbuf, 128 * k)
        if k == 1:
            term[...] = dot(h_t[:, :256], gbuf[:256, :])
        elif k % 2:
            two = slice(128 * k - 128, 128 * k + 128)
            term[...] += dot(h_t[:, two], gbuf[two, :])

    net.reuse(KEYS)
    all_gather(KEYS, gflat, slot, 0, 256, 320, (nothing, nothing, nothing), add_term)

    def columns_of(first, lo, hi):
        rows = pl.ds(pl.multiple_of(first, 64), DSH)
        for j in range(lo, hi):
            yield pl.ds(DSH * j, DSH), term[rows, 128 * j : 128 * j + 128]
        if hi == LT:
            yield pl.ds(DSH * LT, DSH // 2), fold(term[rows, LAT:])

    swaps = []
    for lo, hi, first, last in ((0, 2, 0, 2 * DSH), (2, LT, 2 * DSH, WF)):
        for at_rows, part in columns_of(sib * DSH, lo, hi):
            tsend[at_rows, :] = part.astype(BF)
        flat = pl.ds(first, last - first)
        swaps.append(net.send(tsend.at[flat], trecv.at[flat], twin))

    for copy, lo, hi in zip(swaps, (0, 2), (2, LT), strict=True):
        copy.wait_recv()
        for at_rows, part in columns_of(core * DSH, lo, hi):
            arflat[at_rows, :] = (part + trecv[at_rows, :].astype(F32)).astype(BF)
    arflat[pl.ds(WF, 32 * ZF - WF), :] = jnp.zeros((32 * ZF - WF, 128), BF)

    def part_of(dd):
        return pl.ds(pl.multiple_of(dd * ZF, ZF), ZF)

    def half_of(yy, zz=0, n=NZ * ZF):
        return pl.ds(pl.multiple_of((2 + yy) * NZ * ZF + zz * ZF, ZF), n)

    opposite = {"dp": (1 - yh) * NZ + z}
    level = [lax.rem(z + k, NZ) for k in range(1, NZ)]
    first = net.send(arflat.at[half_of(1 - yh)], far_half, opposite)
    sums_in = [
        net.send(arflat.at[part_of(dd)], arz.at[k], {"dp": dd}) for k, dd in enumerate(sequences)
    ]
    first.wait_recv()
    near_half[...] = (arflat[half_of(yh), :].astype(F32) + far_half[...].astype(F32)).astype(BF)
    level_in = [
        net.send(near_half.at[part_of(zz)], arl.at[k], {"dp": yh * NZ + zz})
        for k, zz in enumerate(level)
    ]
    query_gradient()
    total = near_half[part_of(z), :].astype(F32)
    for k, copy in enumerate(level_in):
        copy.wait_recv()
        total += arl[k].astype(F32)
    net.reuse(KEYS)
    own_rows = half_of(yh, z, ZF)
    agz[own_rows, :] = total.astype(BF)
    level_out = [
        net.send(agz.at[own_rows], agz.at[own_rows], {"dp": yh * NZ + zz}, KEYS) for zz in level
    ]
    total = arflat[part_of(d), :].astype(F32)
    for k, copy in enumerate(sums_in):
        copy.wait_recv()
        total += arz[k].astype(F32)
    agz[part_of(d), :] = total.astype(BF)
    net.reuse(RING)
    sums_out = [
        net.send(agz.at[part_of(d)], agz.at[part_of(d)], {"dp": dd}, RING) for dd in sequences
    ]
    for copy in level_out:
        copy.wait_recv()
    sums_out.append(net.send(agz.at[half_of(yh)], agz.at[half_of(yh)], opposite, KEYS))
    rows_to_heads()
    done = pltpu.make_async_copy(qg_ref, qg_out, local_sems.at[4])
    done.start()
    for copy in sums_out:
        copy.wait_recv()
    done.wait()
    net.finish()
    assert ONCE + net.next[ONCE] == N_SEMS


def hand_over(qg_in, flat, qg_out, wg_ref):
    for j in range(LT):
        wg_ref[:, 128 * j : 128 * j + 128] = flat[pl.ds(DSH * j, DSH), :].astype(F32)
    wg_ref[:, LAT:] = unfold(flat[pl.ds(DSH * LT, DSH // 2), :].astype(F32))
    qg_out[...] = qg_in[...]


def on_device(hidden_in, proj_weight, proj_delta, norm_gain, queries, out_grad, seg_map):
    vmem = pl.BlockSpec(memory_space=pltpu.VMEM)
    freqs = np.float32(ROPE_BASE) ** (-(np.arange(HALF, dtype=np.float32) * 2 / ROPE))
    v = pltpu.VMEM
    scratch = [
        pltpu.SMEM((1, 16), jnp.int32),
        v((NQ, H * KD), BF), v((NQ, H * LAT), BF), v((QR, KD), BF), v((QR, LAT), BF),
        v((ROWS, D), BF), v((2 * ROWS, 8 * 512), BF), v((ROWS, 8 * 512), BF), v((8, WF, 128), BF),
        v((2 * ROWS, KD), F32), v((ROWS, KD), F32), v((ROWS, LAT), F32), v((ROWS, 128), F32),
        v((ROWS, ROPE), F32),
        v((16, KF, 128), BF), v((2048, KD), BF), v((2048, QR), F32), v((2048, QR), F32),
        v((2048, QR), BF), v((2048, QR), BF), v((1, QR), F32), v((1, QR), F32),
        v((8, 1, QR), F32), v((1, QR), F32),
        v((8, 2, KF, 128), F32), v((8, 2, KF, 128), BF), v((8, KF, 128), BF), v((QR, KD), F32),
        v((4, 320, 128), BF), v((4, 320, 128), BF),
        v((2, 2, 128, 128), BF), v((2, 2, 128, 128), BF),
        v((2, 2, 256, 128), BF), v((2, 2, 256, 128), BF),
        v((256, 128), BF), v((256, 128), BF),
        v((2, 160, 128), BF), v((2, 160, 128), BF),
        v((2, 320, 128), BF), v((2, 320, 128), BF),
        v((4, 320, 128), F32),
        v((16, KF, 128), BF), v((1024, KD), BF),
        v((8, ROWS, CHIP), BF), v((CHIP, 1024), BF), v((CHIP, KD), F32),
        v((WF, 128), BF), v((WF, 128), BF),
        v((32 * ZF, 128), BF), v((15, ZF, 128), BF), v((7, ZF, 128), BF), v((8 * ZF, 128), BF),
        v((8 * ZF, 128), BF), v((NQ, H * KD), BF),
        pltpu.SemaphoreType.DMA((N_SEMS,)), pltpu.SemaphoreType.DMA((N_SEMS,)),
        pltpu.SemaphoreType.DMA((5,)),
    ]
    query_grad, flat = pl.pallas_call(
        kernel,
        out_shape=(
            jax.ShapeDtypeStruct((NQ, H * KD), BF),
            jax.ShapeDtypeStruct((32 * ZF, 128), BF),
        ),
        in_specs=[
            pl.BlockSpec(memory_space=pl.ANY),
            pl.BlockSpec(memory_space=pl.ANY),
        ]
        + [vmem] * 4
        + [pl.BlockSpec(memory_space=pl.ANY)] * 2,
        out_specs=(pl.BlockSpec(memory_space=pl.ANY), vmem),
        scratch_shapes=scratch,
        compiler_params=pltpu.CompilerParams(
            collective_id=0, has_side_effects=True, vmem_limit_bytes=60 * 2**20
        ),
        name="mla_backward",
    )(
        seg_map,
        hidden_in[0],
        proj_weight,
        proj_delta,
        norm_gain.reshape(1, LAT),
        jnp.asarray(freqs.astype(np.float32).reshape(1, HALF)),
        queries[0],
        out_grad[0],
    )
    query_grad, weight_grad = pl.pallas_call(
        hand_over,
        out_shape=(
            jax.ShapeDtypeStruct((NQ, H * KD), BF),
            jax.ShapeDtypeStruct((DSH, KD), F32),
        ),
        in_specs=[vmem, vmem],
        out_specs=(vmem, vmem),
        name="hand_over",
    )(query_grad, flat)
    return query_grad.reshape(1, NQ, H * KD), weight_grad


def solution(mesh):
    placed = (
        P("dp", "ctx", None),
        P("ctx", None),
        P("ctx", None),
        P(),
        P("dp", "ctx", None),
        P("dp", "ctx", None),
        P("dp", None),
    )
    return jax.shard_map(
        on_device,
        mesh=mesh,
        in_specs=placed,
        out_specs=(P("dp", "ctx", None), P("ctx", None)),
        check_vma=False,
    )
```

profile of v0, /device:TPU:1, one launch (start us, length us, event | category | flops | bytes accessed | tf_op | source)
XLA Modules:
  0.0 122.8 jit_solution(4195319921851100761)
XLA Ops:
  0.6 119.7 %mla_backward.1 = (bf16[4,73728]{1,0:T(4,128)(2,1)}, bf16[2048,128]{1,0:T(8,128)(2,1)}) custom-call(s32[1,16]{1,0:T(1,128)} %seg_in.1, bf16[128,7168]{1,0:T(8,128)(2,1)} %bitcast.5, bf16[448,576]{1,0:T(8,128)(2,1)} %w_ref.1, bf16[448,576]{1,0:T(8,128)(2,1)} %dw_ref.1, f32[1,512]{1,0:T(1,128)} %bitcast.8, f32[1,32]{1,0:T(1,128)} %constant.2.clone.freq_ref, ...), custom_call_target="tpu_custom_call" | custom-call | tf_op jit(solution)/shard_map/mla_backward/pallas_call | solution.py:674
  120.3 2.5 %hand_over.1 = (bf16[4,73728]{1,0:T(4,128)(2,1)}, f32[448,576]{1,0:T(8,128)}) custom-call(bf16[4,73728]{1,0:T(4,128)(2,1)} %get-tuple-element.6.qg_in, bf16[2048,128]{1,0:T(8,128)(2,1)} %get-tuple-element.7.flat), custom_call_target="tpu_custom_call" | custom-call | tf_op jit(solution)/shard_map/hand_over/pallas_call | solution.py:702
where the time goes:
time: 123 us
  Pallas kernels  122 us (99%)
    pallas_call x1, Pallas kernels, on_device(): pl.pallas_call(kernel, out_shape=(jax.ShapeDtypeStruct((NQ, H * KD), BF),...  120 us
    pallas_call x1, Pallas kernels, on_device(): pl.pallas_call(hand_over, out_shape=(jax.ShapeDtypeStruct((NQ, H * KD), B...  2.47 us

commit v1 on v0

--- a/solution.py
+++ b/solution.py
@@ -95,9 +95,9 @@
 
 
 def kernel(
-    seg_in, hid, w_ref, dw_ref, gain_ref, freq_ref, q_in, g_in,
+    seg_in, hid, w_in, dw_in, gain_in, freq_in, q_in, g_in,
     qg_out, agz,
-    seg, q_raw, g_raw, q_ref, g_ref, own_hid, hidw, hidt, wbuf, acc, prec, unit_ref, inv_ref, trig,
+    seg, w_ref, dw_ref, gain_ref, freq_ref, q_raw, g_raw, q_ref, g_ref, own_hid, hidw, hidt, wbuf, acc, prec, unit_ref, inv_ref, trig,
     kflat, kbuf, e_ref, gp_ref, wt_ref, gs_ref, m_ref, l_ref, mj_ref, rd_ref,
     pf, pb, pr, qacc,
     b1s, b1r, a1s, a1r, a2s, a2r, a3s, a3r, b2s, b2r, b3s, b3r, t_b,
@@ -131,14 +131,31 @@
     peers = [right, left, across, twin] + [{"dp": dd} for dd in sequences]
     for peer in peers:
         pl.semaphore_signal(barrier, inc=1, device_id=peer, device_id_type=MESH)
-    own_hidden = pltpu.make_async_copy(hid, own_hid, local_sems.at[0])
+    own_weights, own_deltas, own_hidden, own_segments, own_gain, own_freqs, own_queries, own_grads = [
+        pltpu.make_async_copy(src, dst, local_sems.at[i])
+        for i, (src, dst) in enumerate(
+            (
+                (w_in, w_ref),
+                (dw_in, dw_ref),
+                (hid, own_hid),
+                (seg_in, seg),
+                (gain_in, gain_ref),
+                (freq_in, freq_ref),
+                (q_in, q_raw),
+                (g_in, g_raw),
+            )
+        )
+    ]
+    own_weights.start()
+    own_deltas.start()
     own_hidden.start()
-    own_queries = pltpu.make_async_copy(q_in, q_raw, local_sems.at[1])
+    own_segments.start()
+    own_gain.start()
+    own_freqs.start()
     own_queries.start()
-    own_grads = pltpu.make_async_copy(g_in, g_raw, local_sems.at[2])
     own_grads.start()
-    own_segments = pltpu.make_async_copy(seg_in, seg, local_sems.at[3])
-    own_segments.start()
+    own_weights.wait()
+    own_deltas.wait()
     perturbed = (w_ref[...].astype(F32) + dw_ref[...].astype(F32)).astype(BF)
     mine = chip(x, y)
     for j in range(LT):
@@ -228,6 +245,8 @@
 
     def hidden_windows():
         own_segments.wait()
+        own_gain.wait()
+        own_freqs.wait()
         angles()
         own_hidden.wait()
         for i in range(NX * NY):
@@ -626,7 +645,7 @@
         copy.wait_recv()
     sums_out.append(net.send(agz.at[half_of(yh)], agz.at[half_of(yh)], opposite, KEYS))
     rows_to_heads()
-    done = pltpu.make_async_copy(qg_ref, qg_out, local_sems.at[4])
+    done = pltpu.make_async_copy(qg_ref, qg_out, local_sems.at[8])
     done.start()
     for copy in sums_out:
         copy.wait_recv()
@@ -636,9 +655,13 @@
 
 
 def hand_over(qg_in, flat, qg_out, wg_ref):
+    i = pl.program_id(0)
+    n = DSH // 2
     for j in range(LT):
-        wg_ref[:, 128 * j : 128 * j + 128] = flat[pl.ds(DSH * j, DSH), :].astype(F32)
-    wg_ref[:, LAT:] = unfold(flat[pl.ds(DSH * LT, DSH // 2), :].astype(F32))
+        rows = pl.ds(pl.multiple_of(DSH * j + n * i, 32), n)
+        wg_ref[:, 128 * j : 128 * j + 128] = flat[rows, :].astype(F32)
+    rope = flat[pl.ds(DSH * LT, n), :].astype(F32)
+    wg_ref[:, LAT:] = jnp.where(i == 0, rope[:, :ROPE], rope[:, ROPE:])
     qg_out[...] = qg_in[...]
 
 
@@ -647,7 +670,8 @@
     freqs = np.float32(ROPE_BASE) ** (-(np.arange(HALF, dtype=np.float32) * 2 / ROPE))
     v = pltpu.VMEM
     scratch = [
-        pltpu.SMEM((1, 16), jnp.int32),
+        pltpu.SMEM((1, 16), jnp.int32), v((DSH, KD), BF), v((DSH, KD), BF), v((1, LAT), F32),
+        v((1, HALF), F32),
         v((NQ, H * KD), BF), v((NQ, H * LAT), BF), v((QR, KD), BF), v((QR, LAT), BF),
         v((ROWS, D), BF), v((2 * ROWS, 8 * 512), BF), v((ROWS, 8 * 512), BF), v((8, WF, 128), BF),
         v((2 * ROWS, KD), F32), v((ROWS, KD), F32), v((ROWS, LAT), F32), v((ROWS, 128), F32),
@@ -669,7 +693,7 @@
         v((32 * ZF, 128), BF), v((15, ZF, 128), BF), v((7, ZF, 128), BF), v((8 * ZF, 128), BF),
         v((8 * ZF, 128), BF), v((NQ, H * KD), BF),
         pltpu.SemaphoreType.DMA((N_SEMS,)), pltpu.SemaphoreType.DMA((N_SEMS,)),
-        pltpu.SemaphoreType.DMA((5,)),
+        pltpu.SemaphoreType.DMA((9,)),
     ]
     query_grad, flat = pl.pallas_call(
         kernel,
@@ -677,12 +701,7 @@
             jax.ShapeDtypeStruct((NQ, H * KD), BF),
             jax.ShapeDtypeStruct((32 * ZF, 128), BF),
         ),
-        in_specs=[
-            pl.BlockSpec(memory_space=pl.ANY),
-            pl.BlockSpec(memory_space=pl.ANY),
-        ]
-        + [vmem] * 4
-        + [pl.BlockSpec(memory_space=pl.ANY)] * 2,
+        in_specs=[pl.BlockSpec(memory_space=pl.ANY)] * 8,
         out_specs=(pl.BlockSpec(memory_space=pl.ANY), vmem),
         scratch_shapes=scratch,
         compiler_params=pltpu.CompilerParams(
@@ -705,8 +724,15 @@
             jax.ShapeDtypeStruct((NQ, H * KD), BF),
             jax.ShapeDtypeStruct((DSH, KD), F32),
         ),
-        in_specs=[vmem, vmem],
-        out_specs=(vmem, vmem),
+        grid=(2,),
+        in_specs=[
+            pl.BlockSpec((NQ, H * KD // 2), lambda i: (0, i)),
+            pl.BlockSpec((32 * ZF, 128), lambda i: (0, 0)),
+        ],
+        out_specs=(
+            pl.BlockSpec((NQ, H * KD // 2), lambda i: (0, i)),
+            pl.BlockSpec((DSH // 2, KD), lambda i: (i, 0)),
+        ),
         name="hand_over",
     )(query_grad, flat)
     return query_grad.reshape(1, NQ, H * KD), weight_grad

time: 123 us -> 121 us (0.984)
  Pallas kernels: 122 us -> 120 us
    pallas_call x1, Pallas kernels: 120 us -> 118 us  [on_device(): pl.pallas_call(kernel, out_shape=(jax.ShapeDtypeStruct((NQ, H * KD), BF),...]
where the time goes in v1:
time: 121 us
  Pallas kernels  120 us (99%)
    pallas_call x1, Pallas kernels, on_device(): pl.pallas_call(kernel, out_shape=(jax.ShapeDtypeStruct((NQ, H * KD), BF),...  118 us

profile of v1, /device:TPU:1, one launch (start us, length us, event | category | flops | bytes accessed | tf_op | source)
XLA Modules:
  0.0 121.1 jit_solution(1963355497594647625)
XLA Ops:
  0.6 118.1 %mla_backward.1 = (bf16[4,73728]{1,0:T(4,128)(2,1)}, bf16[2048,128]{1,0:T(8,128)(2,1)}) custom-call(s32[1,16]{1,0:T(1,128)} %seg_in.1, bf16[128,7168]{1,0:T(8,128)(2,1)} %bitcast.5, bf16[448,576]{1,0:T(8,128)(2,1)} %w_in.1, bf16[448,576]{1,0:T(8,128)(2,1)} %dw_in.1, f32[1,512]{1,0:T(1,128)} %bitcast.8, f32[1,32]{1,0:T(1,128)} %constant.2.clone.freq_in, ...), custom_call_target="tpu_custom_call" | custom-call | tf_op jit(solution)/shard_map/mla_backward/pallas_call | solution.py:698
  118.7 2.4 %hand_over.1 = (bf16[4,73728]{1,0:T(4,128)(2,1)}, f32[448,576]{1,0:T(8,128)}) custom-call(bf16[4,73728]{1,0:T(4,128)(2,1)} %get-tuple-element.6.qg_in, bf16[2048,128]{1,0:T(8,128)(2,1)} %get-tuple-element.7.flat), custom_call_target="tpu_custom_call" | custom-call | tf_op jit(solution)/shard_map/hand_over/pallas_call | solution.py:721
